TPU v7x, 512 devices: a whole 4x8x8 slice. The times are simulated.
512 devices in a mesh: chan: 16 (over z, core), exp: 32 (over x, y).
Axes of the slice: x: 4, y: 8, z: 8, core: 2. Of those that a mesh axis runs over, the one named last changes fastest.
Arguments:
- tokens: bfloat16 [96, 256, 2048], P('chan', 'exp'), may hold values from -6 to 6
- kernel: float32 [3, 3, 2048], replicated, may hold values from -2 to 2
- gain: float32 [2048], replicated, may hold values from 0.1 to 1.9
- routes: int32 [24576, 2], P(('chan', 'exp')), may hold values from 0 to 63, all different within a row; in each aligned block of 48 rows (0 to 47, 48 to 95, ...) at most 2 rows name the same one
- gate_num: int32 [24576, 2], P(('chan', 'exp')), may hold values from 1 to 15
- gate_proj: bfloat16 [512, 176, 2048], P(('exp', 'chan')), may hold values from -0.125 to 0.125
- up_proj: bfloat16 [512, 176, 2048], P(('exp', 'chan')), may hold values from -0.125 to 0.125
- down_proj: bfloat16 [512, 176, 2048], P(('exp', 'chan')), may hold values from -0.15625 to 0.15625
Outputs:
- mixed: bfloat16 [96, 256, 2048], P('chan', 'exp')
Inputs may be any that keep to these rules, and one draw needn't show every extreme that they name: `routes`: the two ids of a row differ. Rows r * 48 to r * 48 + 47 are the tokens of one device, and in each such block no expert is named more than 2 times; some expert is named exactly 2 times in some blocks.
All inputs are finite; a program needn't handle non-finite values.
Results may differ from a plain program's by a relative error of at most 0.0085.
Values may be sent and summed in bfloat16 or wider, within the bound.
A program may use at most 64 MiB of HBM per device.

v0:
```python
import jax
import jax.numpy as jnp
from jax import lax
from jax.sharding import PartitionSpec as P

EXP_DEV = 2
eps = 1e-06


def with_halo(block, sides, width):
    for axis, dim in sides:
        count = lax.axis_size(axis)
        forward = [(i, i + 1) for i in range(count - 1)]
        backward = [(target, source) for source, target in forward]
        low = lax.ppermute(
            lax.slice_in_dim(block, block.shape[dim] - width, None, axis=dim), axis, forward
        )
        high = lax.ppermute(lax.slice_in_dim(block, 0, width, axis=dim), axis, backward)
        block = jnp.concatenate([low, block, high], axis=dim)
    return block


def depthwise(padded, kernel, row_count, col_count):
    image = padded.astype(jnp.float32)
    conv_sum = jnp.zeros((row_count, col_count, image.shape[2]), jnp.float32)
    for row_shift in range(3):
        for col_shift in range(3):
            conv_sum = (
                conv_sum
                + kernel[row_shift, col_shift]
                * image[row_shift : row_shift + row_count, col_shift : col_shift + col_count]
            )
    return conv_sum


def body(tokens, kernel, gain, routes, gate_num, gate_proj, up_proj, down_proj):
    row_count, col_count, width = tokens.shape
    padded = with_halo(tokens, (("chan", 0), ("exp", 1)), 1)
    conv_out = depthwise(padded, kernel, row_count, col_count)
    local_tokens = row_count * col_count
    flat_conv = conv_out.reshape(local_tokens, width)
    inverse_rms = lax.rsqrt(jnp.mean(flat_conv * flat_conv, axis=1, keepdims=True) + eps)
    normed = (flat_conv * inverse_rms * gain).astype(jnp.bfloat16)
    owners = lax.axis_size("exp")
    chan_count = lax.axis_size("chan")
    expert_count = EXP_DEV * owners
    capacity = 3 * local_tokens // expert_count
    slices = chan_count // EXP_DEV
    slot_count = expert_count * capacity
    route_pairs = routes.reshape(-1)
    onehot = (route_pairs[:, None] == jnp.arange(expert_count, dtype=jnp.int32)[None, :]).astype(
        jnp.int32
    )
    earlier = jnp.cumsum(onehot, axis=0) - onehot
    slot_rank = jnp.sum(earlier * onehot, axis=1)
    slot_index = (route_pairs % EXP_DEV * owners + route_pairs // EXP_DEV) * capacity + slot_rank
    chosen = (slot_index[:, None] == jnp.arange(slot_count, dtype=jnp.int32)[None, :]).reshape(
        local_tokens, 2, slot_count
    )
    placing = jnp.sum(chosen.astype(jnp.bfloat16), axis=1)
    outgoing = lax.dot_general(
        placing, normed, (((0,), (0,)), ((), ())), preferred_element_type=jnp.float32
    )
    outgoing = outgoing.astype(jnp.bfloat16).reshape(EXP_DEV, owners, capacity, width)
    arrived = lax.all_to_all(outgoing, "exp", split_axis=1, concat_axis=1, tiled=True)
    half_index = lax.axis_index("chan") // slices
    own_rows = lax.dynamic_index_in_dim(
        lax.all_gather(arrived, "chan", axis=1, tiled=True), half_index, 0, keepdims=False
    )
    block_shape = own_rows.shape
    flat_rows = own_rows.reshape(-1, width)
    gate_val = lax.dot_general(
        flat_rows, gate_proj[0], (((1,), (1,)), ((), ())), preferred_element_type=jnp.float32
    )
    up_val = lax.dot_general(
        flat_rows, up_proj[0], (((1,), (1,)), ((), ())), preferred_element_type=jnp.float32
    )
    hidden = (jax.nn.silu(gate_val) * up_val).astype(jnp.bfloat16)
    down_part = jnp.dot(hidden, down_proj[0], preferred_element_type=jnp.float32).astype(
        jnp.bfloat16
    )
    partial_rows = down_part.reshape(block_shape)
    partial_rows = partial_rows.reshape(chan_count, owners, capacity, width)
    returned = lax.all_to_all(partial_rows, "chan", split_axis=0, concat_axis=0, tiled=True)
    summed = jnp.sum(
        returned.reshape(EXP_DEV, slices, owners, capacity, width).astype(jnp.float32), axis=1
    ).astype(jnp.bfloat16)
    returned_rows = lax.all_to_all(summed, "exp", split_axis=1, concat_axis=1, tiled=True)
    numer = gate_num.astype(jnp.float32)
    fraction = numer / jnp.sum(numer, axis=1, keepdims=True)
    weighting = jnp.sum(chosen.astype(jnp.float32) * fraction[:, :, None], axis=1)
    moe_out = jnp.dot(
        weighting,
        returned_rows.reshape(slot_count, width).astype(jnp.float32),
        precision=lax.Precision.HIGHEST,
    )
    mixed = (flat_conv + moe_out).astype(jnp.bfloat16)
    return mixed.reshape(row_count, col_count, width)


def solution(mesh):
    return jax.shard_map(
        body,
        mesh=mesh,
        in_specs=(
            P("chan", "exp", None),
            P(),
            P(),
            P(("chan", "exp"), None),
            P(("chan", "exp"), None),
            P(("exp", "chan"), None, None),
            P(("exp", "chan"), None, None),
            P(("exp", "chan"), None, None),
        ),
        out_specs=P("chan", "exp", None),
        check_vma=False,
    )
```

profile of v0, /device:TPU:9, one launch (start us, length us, event | category | flops | bytes accessed | tf_op | source)
XLA Modules:
  0.0 289.5 jit_solution(8126721402879814620)
XLA Ops:
  6.5 0.9 fusion.41
  7.4 4.5 %collective-permute-start = (bf16[1,8,2048]{2,1,0:T(8,128)(2,1)S(1)}, bf16[1,8,2048]{2,1,0:T(8,128)(2,1)S(1)}, u32[]{:S(2)}, u32[]{:S(2)}) collective-permute-start(bf16[1,8,2048]{2,1,0:T(8,128)(2,1)S(1)} %get-tuple-element.10), channel_id=1, source_target_pairs={{0,32},{32,64},{64,96},{96,128},{128,160},{160,192},{192,224},{224... | collective-permute-start | bytes 98312 | tf_op jit(solution)/shard_map/ppermute | solution.py:15
  12.0 1.9 collective-permute-start.1
  13.9 0.8 copy.61
  14.7 0.7 broadcast_compare_fusion
  15.3 1.0 fusion.42
  16.7 0.2 select_reduce_fusion.1
  17.3 0.9 constant_dynamic-update-slice_fusion.1
  18.3 3.2 %collective-permute-start.2 = (bf16[8,1,2048]{2,1,0:T(2,128)(2,1)S(1)}, bf16[8,1,2048]{2,1,0:T(2,128)(2,1)S(1)}, u32[]{:S(2)}, u32[]{:S(2)}) collective-permute-start(bf16[8,1,2048]{2,1,0:T(2,128)(2,1)S(1)} %get-tuple-element.7), channel_id=1, source_target_pairs={{0,1},{1,2},{2,3},{3,4},{4,5},{5,6},{6,7},{7,8},{8,9},{9,10},{10,1... | collective-permute-start | bytes 98312 | tf_op jit(solution)/shard_map/ppermute | solution.py:15
  21.6 2.9 %collective-permute-start.3 = (bf16[8,1,2048]{2,1,0:T(2,128)(2,1)S(1)}, bf16[8,1,2048]{2,1,0:T(2,128)(2,1)S(1)}, u32[]{:S(2)}, u32[]{:S(2)}) collective-permute-start(bf16[8,1,2048]{2,1,0:T(2,128)(2,1)S(1)} %get-tuple-element.8), channel_id=1, source_target_pairs={{1,0},{2,1},{3,2},{4,3},{5,4},{6,5},{7,6},{8,7},{9,8},{10,9},{11,1... | collective-permute-start | bytes 98312 | tf_op jit(solution)/shard_map/ppermute | solution.py:18
  24.6 0.2 collective-permute-done.2
  24.8 1.8 collective-permute-done.3
  26.6 0.2 maximum_convert_fusion
  26.8 0.6 multiply_reduce_fusion
  27.5 0.4 convolution_convert_fusion.1
  27.9 0.3 reshape.99
  28.2 0.5 copy.69
  28.8 27.3 %all_to_all.15 = bf16[2,32,2,2048]{3,2,0,1:T(2,128)(2,1)} all-to-all(bf16[2,32,2,2048]{3,2,0,1:T(2,128)(2,1)S(1)} %copy.69), channel_id=1, replica_groups=mesh['chan'=16,'exp'=32] {'exp'}, dimensions={1} | all-to-all | bytes 1048576 | tf_op jit(solution)/shard_map/all_to_all | solution.py:65
  56.1 58.8 %all-gather.2.cloned.1.call-done = bf16[2,512,2,2048]{3,2,0,1:T(2,128)(2,1)} async-done(((bf16[2,32,2,2048]{3,2,0,1:T(2,128)(2,1)}), bf16[2,512,2,2048]{3,2,0,1:T(2,128)(2,1)}) %all-gather.2.cloned.1.call-update) | async-done | bytes 8388624 | tf_op jit(solution)/shard_map/all_gather | solution.py:68
  115.0 7.0 %constant_dynamic-slice_fusion = bf16[1,512,2,2048]{3,2,0,1:T(2,128)(2,1)} fusion(bf16[2,512,2,2048]{3,2,0,1:T(2,128)(2,1)} %all-gather.2.cloned.1.call-done, s32[]{:T(128)S(6)} %select_n.31), kind=kLoop, calls=%fused_computation.70 | loop fusion | bytes 8388612 | tf_op jit(solution)/shard_map/jit(dynamic_index_in_dim)/dynamic_slice | solution.py:67
  122.0 7.3 %reshape.100 = bf16[1024,2048]{1,0:T(8,128)(2,1)} reshape(bf16[1,512,2,2048]{3,2,0,1:T(2,128)(2,1)} %constant_dynamic-slice_fusion) | data formatting | bytes 8388608 | tf_op jit(solution)/shard_map/reshape | solution.py:71
  129.3 4.7 %fusion.6 = f32[1024,176]{0,1:T(8,128)} fusion(bf16[1024,2048]{1,0:T(8,128)(2,1)} %reshape.100, bf16[1,176,2048]{2,1,0:T(8,128)(2,1)S(1)} %copy-done.3), kind=kOutput, calls=%fused_computation.10 | convolution fusion | flops 738197504 | bytes 5636096 | tf_op jit(solution)/shard_map/dot_general | solution.py:72
  134.0 7.1 %convolution_convert_fusion = bf16[1024,2048]{1,0:T(8,128)(2,1)} fusion(bf16[1024,2048]{1,0:T(8,128)(2,1)} %reshape.100, bf16[1,176,2048]{2,1,0:T(8,128)(2,1)S(1)} %copy-done, bf16[1,176,2048]{2,1,0:T(8,128)(2,1)S(1)} %copy-done.4, f32[1024,176]{0,1:T(8,128)} %fusion.6), kind=kOutput, calls=%fused_computation.1 | convolution fusion | flops 1479573504 | bytes 10551296 | tf_op jit(solution)/shard_map/dot_general | solution.py:79
  141.1 7.6 %reshape_reshape.3 = bf16[16,32,2,2048]{3,2,1,0:T(2,128)(2,1)} reshape(bf16[1024,2048]{1,0:T(8,128)(2,1)} %convolution_convert_fusion) | data formatting | bytes 8388608 | tf_op jit(solution)/shard_map/reshape;reshape | solution.py:83
  148.7 100.3 %all_to_all.16 = bf16[16,32,2,2048]{3,2,1,0:T(2,128)(2,1)S(1)} all-to-all(bf16[16,32,2,2048]{3,2,1,0:T(2,128)(2,1)} %reshape_reshape.3), channel_id=1, replica_groups=mesh['chan'=16,'exp'=32] {'chan'}, dimensions={0} | all-to-all | bytes 8388608 | tf_op jit(solution)/shard_map/all_to_all | solution.py:84
  249.0 3.8 %bitcast_reduce_fusion = bf16[2,32,2,2048]{3,2,1,0:T(2,128)(2,1)S(1)} fusion(bf16[16,32,2,2048]{3,2,1,0:T(2,128)(2,1)S(1)} %all_to_all.16), kind=kLoop, calls=%fused_computation | loop fusion | flops 1835008 | bytes 4718592 | tf_op jit(solution)/shard_map/reduce_sum | solution.py:85
  252.9 1.4 copy.70
  254.2 9.3 %all-to-all-start.2 = ((bf16[2,32,2,2048]{3,2,0,1:T(2,128)(2,1)}), bf16[2,32,2,2048]{3,2,0,1:T(2,128)(2,1)S(1)}, u32[]{:S(2)}, u32[]{:S(2)}) async-start(bf16[2,32,2,2048]{3,2,0,1:T(2,128)(2,1)} %copy.70), calls=%async_computation.2 | async-start | bytes 1048576 | tf_op jit(solution)/shard_map/all_to_all | solution.py:88
  263.6 17.4 %all-to-all-done.2 = bf16[2,32,2,2048]{3,2,0,1:T(2,128)(2,1)S(1)} async-done(((bf16[2,32,2,2048]{3,2,0,1:T(2,128)(2,1)}), bf16[2,32,2,2048]{3,2,0,1:T(2,128)(2,1)S(1)}, u32[]{:S(2)}, u32[]{:S(2)}) %all-to-all-start.2) | async-done | bytes 524320 | tf_op jit(solution)/shard_map/all_to_all | solution.py:88
  281.0 0.4 copy.71
  281.4 0.2 reshape.102
  281.6 1.0 fusion.1
  (30 shorter events, 1.1 us)
Async XLA Ops:
  6.5 127.5 %copy-start = (bf16[1,176,2048]{2,1,0:T(8,128)(2,1)S(1)}, bf16[1,176,2048]{2,1,0:T(8,128)(2,1)}, u32[]{:S(2)}) copy-start(bf16[1,176,2048]{2,1,0:T(8,128)(2,1)} %param.15) | copy-start | bytes 2162692
  6.5 21.0 %copy-start.1 = (f32[2048]{0:T(1024)S(1)}, f32[2048]{0:T(1024)}, u32[]{:S(2)}) copy-start(f32[2048]{0:T(1024)} %param.10) | copy-start | bytes 24580
  6.5 108.4 %all-gather.2.cloned.1.call-start = ((), (), s32[]{:S(2)}) async-start(), calls=%async_computation.3 | async-start | bytes 8912896 | tf_op jit(solution)/shard_map/all_gather | solution.py:68
  7.4 9.9 %collective-permute-start = (bf16[1,8,2048]{2,1,0:T(8,128)(2,1)S(1)}, bf16[1,8,2048]{2,1,0:T(8,128)(2,1)S(1)}, u32[]{:S(2)}, u32[]{:S(2)}) collective-permute-start(bf16[1,8,2048]{2,1,0:T(8,128)(2,1)S(1)} %get-tuple-element.10), channel_id=1, source_target_pairs={{0,32},{32,64},{64,96},{96,128},{128,160},{160,192},{192,224},{224... | collective-permute-start | bytes 98312 | tf_op jit(solution)/shard_map/ppermute | solution.py:15
  12.0 6.3 %collective-permute-start.1 = (bf16[1,8,2048]{2,1,0:T(8,128)(2,1)S(1)}, bf16[1,8,2048]{2,1,0:T(8,128)(2,1)S(1)}, u32[]{:S(2)}, u32[]{:S(2)}) collective-permute-start(bf16[1,8,2048]{2,1,0:T(8,128)(2,1)S(1)} %get-tuple-element.9), channel_id=1, source_target_pairs={{32,0},{64,32},{96,64},{128,96},{160,128},{192,160},{224,192},{256... | collective-permute-start | bytes 98312 | tf_op jit(solution)/shard_map/ppermute | solution.py:18
  18.3 6.4 %collective-permute-start.2 = (bf16[8,1,2048]{2,1,0:T(2,128)(2,1)S(1)}, bf16[8,1,2048]{2,1,0:T(2,128)(2,1)S(1)}, u32[]{:S(2)}, u32[]{:S(2)}) collective-permute-start(bf16[8,1,2048]{2,1,0:T(2,128)(2,1)S(1)} %get-tuple-element.7), channel_id=1, source_target_pairs={{0,1},{1,2},{2,3},{3,4},{4,5},{5,6},{6,7},{7,8},{8,9},{9,10},{10,1... | collective-permute-start | bytes 98312 | tf_op jit(solution)/shard_map/ppermute | solution.py:15
  21.6 5.0 %collective-permute-start.3 = (bf16[8,1,2048]{2,1,0:T(2,128)(2,1)S(1)}, bf16[8,1,2048]{2,1,0:T(2,128)(2,1)S(1)}, u32[]{:S(2)}, u32[]{:S(2)}) collective-permute-start(bf16[8,1,2048]{2,1,0:T(2,128)(2,1)S(1)} %get-tuple-element.8), channel_id=1, source_target_pairs={{1,0},{2,1},{3,2},{4,3},{5,4},{6,5},{7,6},{8,7},{9,8},{10,9},{11,1... | collective-permute-start | bytes 98312 | tf_op jit(solution)/shard_map/ppermute | solution.py:18
  122.0 7.3 %copy-start.3 = (bf16[1,176,2048]{2,1,0:T(8,128)(2,1)S(1)}, bf16[1,176,2048]{2,1,0:T(8,128)(2,1)}, u32[]{:S(2)}) copy-start(bf16[1,176,2048]{2,1,0:T(8,128)(2,1)} %param.13) | copy-start | bytes 2162692
  129.3 4.7 %copy-start.4 = (bf16[1,176,2048]{2,1,0:T(8,128)(2,1)S(1)}, bf16[1,176,2048]{2,1,0:T(8,128)(2,1)}, u32[]{:S(2)}) copy-start(bf16[1,176,2048]{2,1,0:T(8,128)(2,1)} %param.14) | copy-start | bytes 2162692
  249.0 14.5 %copy-start.2 = (s32[48,2]{0,1:T(2,128)S(1)}, s32[48,2]{0,1:T(2,128)}, u32[]{:S(2)}) copy-start(s32[48,2]{0,1:T(2,128)} %param.12) | copy-start | bytes 1156
  254.2 26.8 %all-to-all-start.2 = ((bf16[2,32,2,2048]{3,2,0,1:T(2,128)(2,1)}), bf16[2,32,2,2048]{3,2,0,1:T(2,128)(2,1)S(1)}, u32[]{:S(2)}, u32[]{:S(2)}) async-start(bf16[2,32,2,2048]{3,2,0,1:T(2,128)(2,1)} %copy.70), calls=%async_computation.2 | async-start | bytes 1048576 | tf_op jit(solution)/shard_map/all_to_all | solution.py:88
Sparse Core Ops, SparseCore 0:
  56.2 58.6 all-gather.1
where the time goes:
time: 290 us; the launch traced here: 289 us
  blocking collectives  128 us (44%)
  waiting for transfers between devices  78.2 us (27%)
  local copies, waits for them, and re-layouts  29 us (10%)
  starting transfers between devices  21.9 us (8%)
  between operations  13.6 us (5%)
  matrix products  13.2 us (5%)
  other arithmetic  5.98 us (2%)
    all_to_all x1, blocking collectives, body(): lax.all_to_all(partial_rows, 'chan', split_axis=0, concat_axis=0, tiled=T...  100 us
    all_gather x1, waiting for transfers between devices, body(): lax.all_gather(arrived, 'chan', axis=1, tiled=True)  58.8 us
    all_to_all x1, blocking collectives, body(): lax.all_to_all(outgoing, 'exp', split_axis=1, concat_axis=1, tiled=True)  27.3 us
    all_to_all x1, waiting for transfers between devices, body(): lax.all_to_all(summed, 'exp', split_axis=1, concat_axis=1, tiled=True)  17.4 us
    all_to_all x1, starting transfers between devices, body(): lax.all_to_all(summed, 'exp', split_axis=1, concat_axis=1, tiled=True)  9.28 us
    ppermute x2, starting transfers between devices, with_halo(): lax.ppermute(lax.slice_in_dim(block, block.shape[dim] - width, None, axis...  7.75 us
    another operation x1, local copies, waits for them, and re-layouts, body(): partial_rows = partial_rows.reshape(chan_count, owners, capacity, width)  7.62 us
    reshape x1, local copies, waits for them, and re-layouts, body(): flat_rows = own_rows.reshape(-1, width)  7.28 us
  transfers between devices with their start and end apart: 6, of which 4 were waited for; matrix products, arithmetic and copies ran while one was open for 2% of the time, Pallas kernels for 0%

commit v1 on v0

--- a/solution.py
+++ b/solution.py
@@ -5,6 +5,19 @@
 
 EXP_DEV = 2
 eps = 1e-06
+
+
+def ring_gather(x, axis, dim):
+    ways = lax.axis_size(axis)
+    up = [(d, (d + 1) % ways) for d in range(ways)]
+    down = [(d, (d - 1) % ways) for d in range(ways)]
+    earlier, later = ([x], [x])
+    for _ in range(ways // 2):
+        earlier.append(lax.ppermute(earlier[-1], axis, up))
+    for _ in range((ways - 1) // 2):
+        later.append(lax.ppermute(later[-1], axis, down))
+    line = jnp.concatenate([*earlier[::-1], *later[1:]], axis=dim)
+    return jnp.roll(line, (lax.axis_index(axis) - ways // 2) * x.shape[dim], axis=dim)
 
 
 def with_halo(block, sides, width):
@@ -65,7 +78,7 @@
     arrived = lax.all_to_all(outgoing, "exp", split_axis=1, concat_axis=1, tiled=True)
     half_index = lax.axis_index("chan") // slices
     own_rows = lax.dynamic_index_in_dim(
-        lax.all_gather(arrived, "chan", axis=1, tiled=True), half_index, 0, keepdims=False
+        ring_gather(arrived, "chan", 1), half_index, 0, keepdims=False
     )
     block_shape = own_rows.shape
     flat_rows = own_rows.reshape(-1, width)

time: 290 us -> 356 us (1.23)
  local copies, waits for them, and re-layouts: 29 us -> 87 us
  starting transfers between devices: 21.9 us -> 49.3 us
  waiting for transfers between devices: 78.2 us -> 57 us
  blocking collectives: 128 us -> 142 us
  between operations: 13.6 us -> 0.28 us
    all_gather x1 -> x0, waiting for transfers between devices: 58.8 us -> none  [body(): lax.all_gather(arrived, 'chan', axis=1, tiled=True)]
    unnamed x13 -> x70, local copies, waits for them, and re-layouts: 1.74 us -> 58.6 us
    ppermute x0 -> x15, waiting for transfers between devices: none -> 37.6 us  [the longest x8 32.5 us: ring_gather(): earlier.append(lax.ppermute(earlier[-1], axis, up))]
    ppermute x0 -> x15, starting transfers between devices: none -> 32.4 us  [the longest x8 21.3 us: ring_gather(): earlier.append(lax.ppermute(earlier[-1], axis, up))]
    all_to_all x1, blocking collectives: 100 us -> 114 us  [body(): lax.all_to_all(partial_rows, 'chan', split_axis=0, concat_axis=0, tiled=T...]
    all_to_all x1, starting transfers between devices: 9.28 us -> 4.29 us  [body(): lax.all_to_all(summed, 'exp', split_axis=1, concat_axis=1, tiled=True)]
  transfers between devices with their start and end apart: 6 -> 20, of which waited for: 4 -> 16; matrix products, arithmetic and copies ran while one was open for 2% -> 10% of each run, Pallas kernels for 0% -> 0%
where the time goes in v1:
time: 356 us; the launch traced here: 354 us
  blocking collectives  142 us (40%)
  local copies, waits for them, and re-layouts  87 us (24%)
  waiting for transfers between devices  57 us (16%)
  starting transfers between devices  49.3 us (14%)
  matrix products  13.2 us (4%)
  other arithmetic  5.98 us (2%)
    all_to_all x1, blocking collectives, body(): lax.all_to_all(partial_rows, 'chan', split_axis=0, concat_axis=0, tiled=T...  114 us
    unnamed x70, local copies, waits for them, and re-layouts  58.6 us
    ppermute x8, waiting for transfers between devices, ring_gather(): earlier.append(lax.ppermute(earlier[-1], axis, up))  32.5 us
    all_to_all x1, blocking collectives, body(): lax.all_to_all(outgoing, 'exp', split_axis=1, concat_axis=1, tiled=True)  27.2 us
    ppermute x8, starting transfers between devices, ring_gather(): earlier.append(lax.ppermute(earlier[-1], axis, up))  21.3 us
    all_to_all x1, waiting for transfers between devices, body(): lax.all_to_all(summed, 'exp', split_axis=1, concat_axis=1, tiled=True)  17.4 us
    ppermute x7, starting transfers between devices, ring_gather(): later.append(lax.ppermute(later[-1], axis, down))  11.1 us
    ppermute x2, starting transfers between devices, with_halo(): lax.ppermute(lax.slice_in_dim(block, block.shape[dim] - width, None, axis...  7.75 us
  transfers between devices with their start and end apart: 20, of which 16 were waited for; matrix products, arithmetic and copies ran while one was open for 10% of the time, Pallas kernels for 0%

profile of v1, /device:TPU:9, one launch (start us, length us, event | category | flops | bytes accessed | tf_op | source)
XLA Modules:
  0.0 354.2 jit_solution(7514901632915786380)
XLA Ops:
  0.9 4.5 %collective-permute-start = (bf16[1,8,2048]{2,1,0:T(8,128)(2,1)S(1)}, bf16[1,8,2048]{2,1,0:T(8,128)(2,1)S(1)}, u32[]{:S(2)}, u32[]{:S(2)}) collective-permute-start(bf16[1,8,2048]{2,1,0:T(8,128)(2,1)S(1)} %get-tuple-element.10), channel_id=1, source_target_pairs={{0,32},{32,64},{64,96},{96,128},{128,160},{160,192},{192,224},{224... | collective-permute-start | bytes 98312 | tf_op jit(solution)/shard_map/ppermute | solution.py:28
  11.8 3.2 collective-permute-start.2
  15.0 2.9 collective-permute-start.3
  22.9 27.2 %all_to_all.15 = bf16[2,32,2,2048]{3,2,0,1:T(2,128)(2,1)S(1)} all-to-all(bf16[2,32,2,2048]{3,2,0,1:T(2,128)(2,1)S(1)} %copy.69), channel_id=1, replica_groups=mesh['chan'=16,'exp'=32] {'exp'}, dimensions={1} | all-to-all | bytes 1048576 | tf_op jit(solution)/shard_map/all_to_all | solution.py:78
  50.1 3.8 %collective-permute-start.4 = (bf16[2,32,2,2048]{3,2,0,1:T(2,128)(2,1)S(1)}, bf16[2,32,2,2048]{3,2,0,1:T(2,128)(2,1)S(1)}, u32[]{:S(2)}, u32[]{:S(2)}) collective-permute-start(bf16[2,32,2,2048]{3,2,0,1:T(2,128)(2,1)S(1)} %all_to_all.15), channel_id=1, source_target_pairs={{0,32},{32,64},{64,96},{96,128},{128,160},{160,192},{192,224},{224... | collective-permute-start | bytes 1572872 | tf_op jit(solution)/shard_map/ppermute | solution.py:16
  53.9 6.1 %collective-permute-done.4 = bf16[2,32,2,2048]{3,2,0,1:T(2,128)(2,1)S(1)} collective-permute-done((bf16[2,32,2,2048]{3,2,0,1:T(2,128)(2,1)S(1)}, bf16[2,32,2,2048]{3,2,0,1:T(2,128)(2,1)S(1)}, u32[]{:S(2)}, u32[]{:S(2)}) %collective-permute-start.4) | collective-permute-done | bytes 524320 | tf_op jit(solution)/shard_map/ppermute | solution.py:16
  60.1 2.5 collective-permute-start.5
  62.6 6.1 %collective-permute-done.5 = bf16[2,32,2,2048]{3,2,0,1:T(2,128)(2,1)S(1)} collective-permute-done((bf16[2,32,2,2048]{3,2,0,1:T(2,128)(2,1)S(1)}, bf16[2,32,2,2048]{3,2,0,1:T(2,128)(2,1)S(1)}, u32[]{:S(2)}, u32[]{:S(2)}) %collective-permute-start.5) | collective-permute-done | bytes 524320 | tf_op jit(solution)/shard_map/ppermute | solution.py:16
  68.7 2.5 collective-permute-start.6
  71.2 6.1 %collective-permute-done.6 = bf16[2,32,2,2048]{3,2,0,1:T(2,128)(2,1)S(1)} collective-permute-done((bf16[2,32,2,2048]{3,2,0,1:T(2,128)(2,1)S(1)}, bf16[2,32,2,2048]{3,2,0,1:T(2,128)(2,1)S(1)}, u32[]{:S(2)}, u32[]{:S(2)}) %collective-permute-start.6) | collective-permute-done | bytes 524320 | tf_op jit(solution)/shard_map/ppermute | solution.py:16
  77.3 2.5 collective-permute-start.7
  80.7 5.2 %collective-permute-done.7 = bf16[2,32,2,2048]{3,2,0,1:T(2,128)(2,1)S(1)} collective-permute-done((bf16[2,32,2,2048]{3,2,0,1:T(2,128)(2,1)S(1)}, bf16[2,32,2,2048]{3,2,0,1:T(2,128)(2,1)S(1)}, u32[]{:S(2)}, u32[]{:S(2)}) %collective-permute-start.7) | collective-permute-done | bytes 524320 | tf_op jit(solution)/shard_map/ppermute | solution.py:16
  85.9 2.5 collective-permute-start.8
  90.1 4.4 %collective-permute-done.8 = bf16[2,32,2,2048]{3,2,0,1:T(2,128)(2,1)S(1)} collective-permute-done((bf16[2,32,2,2048]{3,2,0,1:T(2,128)(2,1)S(1)}, bf16[2,32,2,2048]{3,2,0,1:T(2,128)(2,1)S(1)}, u32[]{:S(2)}, u32[]{:S(2)}) %collective-permute-start.8) | collective-permute-done | bytes 524320 | tf_op jit(solution)/shard_map/ppermute | solution.py:16
  94.5 2.5 collective-permute-start.9
  100.8 2.4 collective-permute-done.9
  103.1 2.5 collective-permute-start.10
  107.4 3.0 collective-permute-start.17
  111.7 2.6 collective-permute-start.11
  116.6 4.0 %collective-permute-start.18 = (bf16[2,32,2,2048]{3,2,0,1:T(2,128)(2,1)}, bf16[2,32,2,2048]{3,2,0,1:T(2,128)(2,1)S(1)}, u32[]{:S(2)}, u32[]{:S(2)}) collective-permute-start(bf16[2,32,2,2048]{3,2,0,1:T(2,128)(2,1)} %collective-permute-done.17), channel_id=1, source_target_pairs={{0,480},{32,0},{64,32},{96,64},{128,96},{160,128},{192,160},{224,1... | collective-permute-start | bytes 1572872 | tf_op jit(solution)/shard_map/ppermute | solution.py:18
  128.2 2.3 constant_dynamic-update-slice_fusion.31
  153.8 2.3 constant_dynamic-update-slice_fusion.18
  172.3 2.5 constant_dynamic-update-slice_fusion.5
  178.3 7.0 %constant_dynamic-slice_fusion = bf16[1,512,2,2048]{3,2,0,1:T(2,128)(2,1)} fusion(bf16[2,1024,2,2048]{3,2,0,1:T(2,128)(2,1)} %constant_dynamic-update-slice_fusion.3, s32[]{:T(128)S(6)} %select_n.48, s32[]{:T(128)S(6)} %select_n.51), kind=kLoop, calls=%fused_computation.97 | loop fusion | bytes 8388616 | tf_op jit(solution)/shard_map/jit(dynamic_index_in_dim)/dynamic_slice | solution.py:80
  185.3 7.2 %reshape.100 = bf16[1024,2048]{1,0:T(8,128)(2,1)} reshape(bf16[1,512,2,2048]{3,2,0,1:T(2,128)(2,1)} %constant_dynamic-slice_fusion) | data formatting | bytes 8388608 | tf_op jit(solution)/shard_map/reshape | solution.py:84
  192.5 3.9 %fusion.3 = f32[1024,176]{0,1:T(8,128)S(1)} fusion(bf16[1024,2048]{1,0:T(8,128)(2,1)} %reshape.100, bf16[1,176,2048]{2,1,0:T(8,128)(2,1)} %param.14), kind=kOutput, calls=%fused_computation.7 | convolution fusion | flops 738197504 | bytes 5636096 | tf_op jit(solution)/shard_map/dot_general | solution.py:88
  196.4 7.2 %convolution_convert_fusion = bf16[1024,2048]{1,0:T(8,128)(2,1)} fusion(bf16[1,176,2048]{2,1,0:T(8,128)(2,1)S(1)} %copy-done, f32[1024,176]{0,1:T(8,128)S(1)} %fusion.3, bf16[1024,2048]{1,0:T(8,128)(2,1)} %reshape.100, bf16[1,176,2048]{2,1,0:T(8,128)(2,1)} %param.13), kind=kOutput, calls=%fused_computation.1 | convolution fusion | flops 1479573504 | bytes 10551296 | tf_op jit(solution)/shard_map/dot_general | solution.py:92
  203.6 7.6 %reshape_reshape.3 = bf16[16,32,2,2048]{3,2,1,0:T(2,128)(2,1)} reshape(bf16[1024,2048]{1,0:T(8,128)(2,1)} %convolution_convert_fusion) | data formatting | bytes 8388608 | tf_op jit(solution)/shard_map/reshape;reshape | solution.py:96
  211.2 114.4 %all_to_all.16 = bf16[16,32,2,2048]{3,2,1,0:T(2,128)(2,1)S(1)} all-to-all(bf16[16,32,2,2048]{3,2,1,0:T(2,128)(2,1)} %reshape_reshape.3), channel_id=1, replica_groups=mesh['chan'=16,'exp'=32] {'chan'}, dimensions={0} | all-to-all | bytes 8388608 | tf_op jit(solution)/shard_map/all_to_all | solution.py:97
  325.6 3.8 %bitcast_reduce_fusion = bf16[2,32,2,2048]{3,2,1,0:T(2,128)(2,1)S(1)} fusion(bf16[16,32,2,2048]{3,2,1,0:T(2,128)(2,1)S(1)} %all_to_all.16), kind=kLoop, calls=%fused_computation | loop fusion | flops 1835008 | bytes 4718592 | tf_op jit(solution)/shard_map/reduce_sum | solution.py:98
  330.8 4.3 %all-to-all-start.2 = ((bf16[2,32,2,2048]{3,2,0,1:T(2,128)(2,1)}), bf16[2,32,2,2048]{3,2,0,1:T(2,128)(2,1)S(1)}, u32[]{:S(2)}, u32[]{:S(2)}) async-start(bf16[2,32,2,2048]{3,2,0,1:T(2,128)(2,1)} %copy.70), calls=%async_computation.2 | async-start | bytes 1048576 | tf_op jit(solution)/shard_map/all_to_all | solution.py:101
  335.2 17.4 %all-to-all-done.2 = bf16[2,32,2,2048]{3,2,0,1:T(2,128)(2,1)S(1)} async-done(((bf16[2,32,2,2048]{3,2,0,1:T(2,128)(2,1)}), bf16[2,32,2,2048]{3,2,0,1:T(2,128)(2,1)S(1)}, u32[]{:S(2)}, u32[]{:S(2)}) %all-to-all-start.2) | async-done | bytes 524320 | tf_op jit(solution)/shard_map/all_to_all | solution.py:101
  (115 shorter events, 77.5 us)
Async XLA Ops:
  0.0 196.4 %copy-start = (bf16[1,176,2048]{2,1,0:T(8,128)(2,1)S(1)}, bf16[1,176,2048]{2,1,0:T(8,128)(2,1)}, u32[]{:S(2)}) copy-start(bf16[1,176,2048]{2,1,0:T(8,128)(2,1)} %param.15) | copy-start | bytes 2162692
  0.9 9.9 %collective-permute-start = (bf16[1,8,2048]{2,1,0:T(8,128)(2,1)S(1)}, bf16[1,8,2048]{2,1,0:T(8,128)(2,1)S(1)}, u32[]{:S(2)}, u32[]{:S(2)}) collective-permute-start(bf16[1,8,2048]{2,1,0:T(8,128)(2,1)S(1)} %get-tuple-element.10), channel_id=1, source_target_pairs={{0,32},{32,64},{64,96},{96,128},{128,160},{160,192},{192,224},{224... | collective-permute-start | bytes 98312 | tf_op jit(solution)/shard_map/ppermute | solution.py:28
  5.4 6.3 %collective-permute-start.1 = (bf16[1,8,2048]{2,1,0:T(8,128)(2,1)S(1)}, bf16[1,8,2048]{2,1,0:T(8,128)(2,1)S(1)}, u32[]{:S(2)}, u32[]{:S(2)}) collective-permute-start(bf16[1,8,2048]{2,1,0:T(8,128)(2,1)S(1)} %get-tuple-element.9), channel_id=1, source_target_pairs={{32,0},{64,32},{96,64},{128,96},{160,128},{192,160},{224,192},{256... | collective-permute-start | bytes 98312 | tf_op jit(solution)/shard_map/ppermute | solution.py:31
  11.8 6.4 %collective-permute-start.2 = (bf16[8,1,2048]{2,1,0:T(2,128)(2,1)S(1)}, bf16[8,1,2048]{2,1,0:T(2,128)(2,1)S(1)}, u32[]{:S(2)}, u32[]{:S(2)}) collective-permute-start(bf16[8,1,2048]{2,1,0:T(2,128)(2,1)S(1)} %get-tuple-element.7), channel_id=1, source_target_pairs={{0,1},{1,2},{2,3},{3,4},{4,5},{5,6},{6,7},{7,8},{8,9},{9,10},{10,1... | collective-permute-start | bytes 98312 | tf_op jit(solution)/shard_map/ppermute | solution.py:28
  15.0 5.0 %collective-permute-start.3 = (bf16[8,1,2048]{2,1,0:T(2,128)(2,1)S(1)}, bf16[8,1,2048]{2,1,0:T(2,128)(2,1)S(1)}, u32[]{:S(2)}, u32[]{:S(2)}) collective-permute-start(bf16[8,1,2048]{2,1,0:T(2,128)(2,1)S(1)} %get-tuple-element.8), channel_id=1, source_target_pairs={{1,0},{2,1},{3,2},{4,3},{5,4},{6,5},{7,6},{8,7},{9,8},{10,9},{11,1... | collective-permute-start | bytes 98312 | tf_op jit(solution)/shard_map/ppermute | solution.py:31
  50.1 9.9 %collective-permute-start.4 = (bf16[2,32,2,2048]{3,2,0,1:T(2,128)(2,1)S(1)}, bf16[2,32,2,2048]{3,2,0,1:T(2,128)(2,1)S(1)}, u32[]{:S(2)}, u32[]{:S(2)}) collective-permute-start(bf16[2,32,2,2048]{3,2,0,1:T(2,128)(2,1)S(1)} %all_to_all.15), channel_id=1, source_target_pairs={{0,32},{32,64},{64,96},{96,128},{128,160},{160,192},{192,224},{224... | collective-permute-start | bytes 1572872 | tf_op jit(solution)/shard_map/ppermute | solution.py:16
  60.1 8.6 %collective-permute-start.5 = (bf16[2,32,2,2048]{3,2,0,1:T(2,128)(2,1)S(1)}, bf16[2,32,2,2048]{3,2,0,1:T(2,128)(2,1)S(1)}, u32[]{:S(2)}, u32[]{:S(2)}) collective-permute-start(bf16[2,32,2,2048]{3,2,0,1:T(2,128)(2,1)S(1)} %collective-permute-done.4), channel_id=1, source_target_pairs={{0,32},{32,64},{64,96},{96,128},{128,160},{160,192},{192,224},{224... | collective-permute-start | bytes 1572872 | tf_op jit(solution)/shard_map/ppermute | solution.py:16
  62.6 8.6 %collective-permute-start.12 = (bf16[2,32,2,2048]{3,2,0,1:T(2,128)(2,1)S(1)}, bf16[2,32,2,2048]{3,2,0,1:T(2,128)(2,1)S(1)}, u32[]{:S(2)}, u32[]{:S(2)}) collective-permute-start(bf16[2,32,2,2048]{3,2,0,1:T(2,128)(2,1)S(1)} %all_to_all.15), channel_id=1, source_target_pairs={{0,480},{32,0},{64,32},{96,64},{128,96},{160,128},{192,160},{224,1... | collective-permute-start | bytes 1572872 | tf_op jit(solution)/shard_map/ppermute | solution.py:18
  68.7 8.6 %collective-permute-start.6 = (bf16[2,32,2,2048]{3,2,0,1:T(2,128)(2,1)S(1)}, bf16[2,32,2,2048]{3,2,0,1:T(2,128)(2,1)S(1)}, u32[]{:S(2)}, u32[]{:S(2)}) collective-permute-start(bf16[2,32,2,2048]{3,2,0,1:T(2,128)(2,1)S(1)} %collective-permute-done.5), channel_id=1, source_target_pairs={{0,32},{32,64},{64,96},{96,128},{128,160},{160,192},{192,224},{224... | collective-permute-start | bytes 1572872 | tf_op jit(solution)/shard_map/ppermute | solution.py:16
  71.2 8.7 %collective-permute-start.13 = (bf16[2,32,2,2048]{3,2,0,1:T(2,128)(2,1)S(1)}, bf16[2,32,2,2048]{3,2,0,1:T(2,128)(2,1)S(1)}, u32[]{:S(2)}, u32[]{:S(2)}) collective-permute-start(bf16[2,32,2,2048]{3,2,0,1:T(2,128)(2,1)S(1)} %collective-permute-done.12), channel_id=1, source_target_pairs={{0,480},{32,0},{64,32},{96,64},{128,96},{160,128},{192,160},{224,1... | collective-permute-start | bytes 1572872 | tf_op jit(solution)/shard_map/ppermute | solution.py:18
  77.3 8.6 %collective-permute-start.7 = (bf16[2,32,2,2048]{3,2,0,1:T(2,128)(2,1)S(1)}, bf16[2,32,2,2048]{3,2,0,1:T(2,128)(2,1)S(1)}, u32[]{:S(2)}, u32[]{:S(2)}) collective-permute-start(bf16[2,32,2,2048]{3,2,0,1:T(2,128)(2,1)S(1)} %collective-permute-done.6), channel_id=1, source_target_pairs={{0,32},{32,64},{64,96},{96,128},{128,160},{160,192},{192,224},{224... | collective-permute-start | bytes 1572872 | tf_op jit(solution)/shard_map/ppermute | solution.py:16
  79.9 8.9 %collective-permute-start.14 = (bf16[2,32,2,2048]{3,2,0,1:T(2,128)(2,1)S(1)}, bf16[2,32,2,2048]{3,2,0,1:T(2,128)(2,1)S(1)}, u32[]{:S(2)}, u32[]{:S(2)}) collective-permute-start(bf16[2,32,2,2048]{3,2,0,1:T(2,128)(2,1)S(1)} %collective-permute-done.13), channel_id=1, source_target_pairs={{0,480},{32,0},{64,32},{96,64},{128,96},{160,128},{192,160},{224,1... | collective-permute-start | bytes 1572872 | tf_op jit(solution)/shard_map/ppermute | solution.py:18
  85.9 21.5 %copy-start.11 = (bf16[2,32,2,2048]{3,2,0,1:T(2,128)(2,1)}, bf16[2,32,2,2048]{3,2,0,1:T(2,128)(2,1)S(1)}, u32[]{:S(2)}) copy-start(bf16[2,32,2,2048]{3,2,0,1:T(2,128)(2,1)S(1)} %collective-permute-done.7) | copy-start | bytes 1572868
  85.9 8.6 %collective-permute-start.8 = (bf16[2,32,2,2048]{3,2,0,1:T(2,128)(2,1)S(1)}, bf16[2,32,2,2048]{3,2,0,1:T(2,128)(2,1)S(1)}, u32[]{:S(2)}, u32[]{:S(2)}) collective-permute-start(bf16[2,32,2,2048]{3,2,0,1:T(2,128)(2,1)S(1)} %collective-permute-done.7), channel_id=1, source_target_pairs={{0,32},{32,64},{64,96},{96,128},{128,160},{160,192},{192,224},{224... | collective-permute-start | bytes 1572872 | tf_op jit(solution)/shard_map/ppermute | solution.py:16
  88.8 8.9 %collective-permute-start.15 = (bf16[2,32,2,2048]{3,2,0,1:T(2,128)(2,1)S(1)}, bf16[2,32,2,2048]{3,2,0,1:T(2,128)(2,1)S(1)}, u32[]{:S(2)}, u32[]{:S(2)}) collective-permute-start(bf16[2,32,2,2048]{3,2,0,1:T(2,128)(2,1)S(1)} %collective-permute-done.14), channel_id=1, source_target_pairs={{0,480},{32,0},{64,32},{96,64},{128,96},{160,128},{192,160},{224,1... | collective-permute-start | bytes 1572872 | tf_op jit(solution)/shard_map/ppermute | solution.py:18
  94.5 15.9 %copy-start.13 = (bf16[2,32,2,2048]{3,2,0,1:T(2,128)(2,1)}, bf16[2,32,2,2048]{3,2,0,1:T(2,128)(2,1)S(1)}, u32[]{:S(2)}) copy-start(bf16[2,32,2,2048]{3,2,0,1:T(2,128)(2,1)S(1)} %collective-permute-done.8) | copy-start | bytes 1572868
  94.5 8.6 %collective-permute-start.9 = (bf16[2,32,2,2048]{3,2,0,1:T(2,128)(2,1)S(1)}, bf16[2,32,2,2048]{3,2,0,1:T(2,128)(2,1)S(1)}, u32[]{:S(2)}, u32[]{:S(2)}) collective-permute-start(bf16[2,32,2,2048]{3,2,0,1:T(2,128)(2,1)S(1)} %collective-permute-done.8), channel_id=1, source_target_pairs={{0,32},{32,64},{64,96},{96,128},{128,160},{160,192},{192,224},{224... | collective-permute-start | bytes 1572872 | tf_op jit(solution)/shard_map/ppermute | solution.py:16
  98.5 8.9 %collective-permute-start.16 = (bf16[2,32,2,2048]{3,2,0,1:T(2,128)(2,1)S(1)}, bf16[2,32,2,2048]{3,2,0,1:T(2,128)(2,1)}, u32[]{:S(2)}, u32[]{:S(2)}) collective-permute-start(bf16[2,32,2,2048]{3,2,0,1:T(2,128)(2,1)S(1)} %collective-permute-done.15), channel_id=1, source_target_pairs={{0,480},{32,0},{64,32},{96,64},{128,96},{160,128},{192,160},{224,1... | collective-permute-start | bytes 1572872 | tf_op jit(solution)/shard_map/ppermute | solution.py:18
  103.1 8.6 %collective-permute-start.10 = (bf16[2,32,2,2048]{3,2,0,1:T(2,128)(2,1)S(1)}, bf16[2,32,2,2048]{3,2,0,1:T(2,128)(2,1)}, u32[]{:S(2)}, u32[]{:S(2)}) collective-permute-start(bf16[2,32,2,2048]{3,2,0,1:T(2,128)(2,1)S(1)} %collective-permute-done.9), channel_id=1, source_target_pairs={{0,32},{32,64},{64,96},{96,128},{128,160},{160,192},{192,224},{224... | collective-permute-start | bytes 1572872 | tf_op jit(solution)/shard_map/ppermute | solution.py:16
  107.4 9.2 %collective-permute-start.17 = (bf16[2,32,2,2048]{3,2,0,1:T(2,128)(2,1)}, bf16[2,32,2,2048]{3,2,0,1:T(2,128)(2,1)}, u32[]{:S(2)}, u32[]{:S(2)}) collective-permute-start(bf16[2,32,2,2048]{3,2,0,1:T(2,128)(2,1)} %collective-permute-done.16), channel_id=1, source_target_pairs={{0,480},{32,0},{64,32},{96,64},{128,96},{160,128},{192,160},{224,1... | collective-permute-start | bytes 1572872 | tf_op jit(solution)/shard_map/ppermute | solution.py:18
  111.7 9.7 %collective-permute-start.11 = (bf16[2,32,2,2048]{3,2,0,1:T(2,128)(2,1)}, bf16[2,32,2,2048]{3,2,0,1:T(2,128)(2,1)}, u32[]{:S(2)}, u32[]{:S(2)}) collective-permute-start(bf16[2,32,2,2048]{3,2,0,1:T(2,128)(2,1)} %collective-permute-done.10), channel_id=1, source_target_pairs={{0,32},{32,64},{64,96},{96,128},{128,160},{160,192},{192,224},{224... | collective-permute-start | bytes 1572872 | tf_op jit(solution)/shard_map/ppermute | solution.py:16
  114.3 44.1 %copy-start.16 = (bf16[2,32,2,2048]{3,2,0,1:T(2,128)(2,1)S(1)}, bf16[2,32,2,2048]{3,2,0,1:T(2,128)(2,1)}, u32[]{:S(2)}) copy-start(bf16[2,32,2,2048]{3,2,0,1:T(2,128)(2,1)} %copy-done.15) | copy-start | bytes 1572868
  114.3 45.4 %copy-start.14 = (bf16[2,32,2,2048]{3,2,0,1:T(2,128)(2,1)S(1)}, bf16[2,32,2,2048]{3,2,0,1:T(2,128)(2,1)}, u32[]{:S(2)}) copy-start(bf16[2,32,2,2048]{3,2,0,1:T(2,128)(2,1)} %copy-done.13) | copy-start | bytes 1572868
  114.3 46.6 %copy-start.12 = (bf16[2,32,2,2048]{3,2,0,1:T(2,128)(2,1)S(1)}, bf16[2,32,2,2048]{3,2,0,1:T(2,128)(2,1)}, u32[]{:S(2)}) copy-start(bf16[2,32,2,2048]{3,2,0,1:T(2,128)(2,1)} %copy-done.11) | copy-start | bytes 1572868
  114.3 47.9 %copy-start.6 = (bf16[2,32,2,2048]{3,2,0,1:T(2,128)(2,1)S(1)}, bf16[2,32,2,2048]{3,2,0,1:T(2,128)(2,1)}, u32[]{:S(2)}) copy-start(bf16[2,32,2,2048]{3,2,0,1:T(2,128)(2,1)} %copy-done.5) | copy-start | bytes 1572868
  114.3 49.1 %copy-start.2 = (bf16[2,32,2,2048]{3,2,0,1:T(2,128)(2,1)S(1)}, bf16[2,32,2,2048]{3,2,0,1:T(2,128)(2,1)}, u32[]{:S(2)}) copy-start(bf16[2,32,2,2048]{3,2,0,1:T(2,128)(2,1)} %copy-done.1) | copy-start | bytes 1572868
  114.3 54.2 %copy-start.4 = (bf16[2,32,2,2048]{3,2,0,1:T(2,128)(2,1)S(1)}, bf16[2,32,2,2048]{3,2,0,1:T(2,128)(2,1)}, u32[]{:S(2)}) copy-start(bf16[2,32,2,2048]{3,2,0,1:T(2,128)(2,1)} %copy-done.3) | copy-start | bytes 1572868
  114.3 55.5 %copy-start.8 = (bf16[2,32,2,2048]{3,2,0,1:T(2,128)(2,1)S(1)}, bf16[2,32,2,2048]{3,2,0,1:T(2,128)(2,1)}, u32[]{:S(2)}) copy-start(bf16[2,32,2,2048]{3,2,0,1:T(2,128)(2,1)} %copy-done.7) | copy-start | bytes 1572868
  114.4 56.7 %copy-start.10 = (bf16[2,32,2,2048]{3,2,0,1:T(2,128)(2,1)S(1)}, bf16[2,32,2,2048]{3,2,0,1:T(2,128)(2,1)}, u32[]{:S(2)}) copy-start(bf16[2,32,2,2048]{3,2,0,1:T(2,128)(2,1)} %copy-done.9) | copy-start | bytes 1572868
  116.6 35.9 %collective-permute-start.18 = (bf16[2,32,2,2048]{3,2,0,1:T(2,128)(2,1)}, bf16[2,32,2,2048]{3,2,0,1:T(2,128)(2,1)S(1)}, u32[]{:S(2)}, u32[]{:S(2)}) collective-permute-start(bf16[2,32,2,2048]{3,2,0,1:T(2,128)(2,1)} %collective-permute-done.17), channel_id=1, source_target_pairs={{0,480},{32,0},{64,32},{96,64},{128,96},{160,128},{192,160},{224,1... | collective-permute-start | bytes 1572872 | tf_op jit(solution)/shard_map/ppermute | solution.py:18
  196.4 138.7 %copy-start.17 = (s32[48,2]{0,1:T(2,128)S(1)}, s32[48,2]{0,1:T(2,128)}, u32[]{:S(2)}) copy-start(s32[48,2]{0,1:T(2,128)} %param.12) | copy-start | bytes 1156
  330.8 21.8 %all-to-all-start.2 = ((bf16[2,32,2,2048]{3,2,0,1:T(2,128)(2,1)}), bf16[2,32,2,2048]{3,2,0,1:T(2,128)(2,1)S(1)}, u32[]{:S(2)}, u32[]{:S(2)}) async-start(bf16[2,32,2,2048]{3,2,0,1:T(2,128)(2,1)} %copy.70), calls=%async_computation.2 | async-start | bytes 1048576 | tf_op jit(solution)/shard_map/all_to_all | solution.py:101
  (6 other events, 34.2 us)
